TPU v7x, 256 devices: a whole 4x4x8 slice. The times are simulated.
256 devices in a mesh: ctx: 16 (over z, x_lo), wt: 4 (over x_hi, core), head: 4 (over y).
Axes of the slice: x: 4 (x_hi: 2, x_lo: 2; x = x_hi * 2 + x_lo), y: 4, z: 8, core: 2. Of those that a mesh axis runs over, the one named last changes fastest.
Arguments:
- query_compressed: bfloat16 [2, 1024, 1536], P(None, 'ctx', 'wt'), may hold values from -6 to 6
- query_gain: float32 [1536], replicated, may hold values from 0.25 to 1.75
- w_query: bfloat16 [1536, 24576], P(None, ('wt', 'head')), may hold values from -0.15625 to 0.15625
- new_latent: bfloat16 [2, 1024, 576], P(None, 'ctx'), may hold values from -6 to 6
- latent_gain: float32 [512], replicated, may hold values from 0.25 to 1.75
- cache: bfloat16 [2, 4096, 576], P(None, 'ctx'), may hold values from -1100 to 1100
- prefix_len: int32 [2], replicated, may hold values from 1024 to 4096, as said below
- w_key_up: bfloat16 [128, 512, 128], P(('wt', 'head'), 'ctx'), may hold values from -0.5 to 0.5
- w_value_up: bfloat16 [128, 512, 128], P(('wt', 'head'), 'ctx'), may hold values from -4 to 4
Outputs:
- attended: bfloat16 [2, 1024, 16384], P(None, 'ctx', ('wt', 'head'))
Inputs may be any that keep to these rules, and one draw needn't show every extreme that they name: `prefix_len`: one prompt's prefix fills all 4096 cache slots.
All inputs are finite; a program needn't handle non-finite values.
Results may differ from a plain program's by a relative error of at most 0.029.
Values may be sent and summed in bfloat16 or wider, within the bound.
A program may use at most 128 MiB of HBM per device.

v0:
```python
import jax
import jax.numpy as jnp
from jax import lax
from jax.sharding import PartitionSpec as P

eps = 1e-06
rope_base = 10000.0


def rms_scale(values, gain_vector):
    mean_square = jnp.mean(values * values, axis=-1, keepdims=True)
    return values * lax.rsqrt(mean_square + eps) * gain_vector


def rotate(values, positions):
    half_width = values.shape[-1] // 2
    exponent = jnp.arange(half_width, dtype=jnp.float32) * (-2.0 / values.shape[-1])
    frequency = jnp.exp(exponent * jnp.log(jnp.float32(rope_base)))
    angles = positions[..., None] * frequency
    cosine = jnp.cos(angles)
    sine_values = jnp.sin(angles)
    leading = values[..., :half_width]
    trailing = values[..., half_width:]
    return jnp.concatenate(
        [leading * cosine - trailing * sine_values, trailing * cosine + leading * sine_values], -1
    )


def visibility(shard_index, offset, cache_rows, fresh_rows, prefix_len, local_tok):
    is_cache = offset < cache_rows
    slot_index = shard_index * cache_rows + offset
    token_index = shard_index * fresh_rows + offset - cache_rows
    cache_ok = is_cache[None, :] & (slot_index[None, :] < prefix_len[:, None])
    fresh_ok = jnp.logical_not(is_cache)[None, :] & (token_index[None, :] <= local_tok[:, None])
    return cache_ok[:, None, :] | fresh_ok[None, :, :]


def attend(running, portion, visible, q_lat, q_rope, kv_width, score_scale):
    running_max, weight_sum, accumulated = running
    latent = portion[..., :kv_width]
    scores = jnp.einsum("sgqc,snc->sgqn", q_lat, latent, preferred_element_type=jnp.float32)
    scores = scores + jnp.einsum(
        "sgqr,snr->sgqn", q_rope, portion[..., kv_width:], preferred_element_type=jnp.float32
    )
    visible_mask = visible[:, None, :, :]
    scores = jnp.where(visible_mask, scores * score_scale, -1e30)
    new_max = jnp.maximum(running_max, jnp.max(scores, axis=-1))
    weights = jnp.where(visible_mask, jnp.exp(scores - new_max[..., None]), 0.0)
    weight_sum = jnp.sum(weights, axis=-1)
    update = jnp.einsum(
        "sgqn,snc->sgqc", weights.astype(jnp.bfloat16), latent, preferred_element_type=jnp.float32
    )
    accumulated = update
    return (new_max, weight_sum, accumulated)


def shards(
    query_compressed,
    query_gain,
    w_query,
    new_latent,
    latent_gain,
    cache,
    prefix_len,
    w_key_up,
    w_value_up,
):
    prompts = new_latent.shape[0]
    fresh_rows = new_latent.shape[1]
    cache_rows = cache.shape[1]
    kv_width = latent_gain.shape[0]
    rope_width = cache.shape[2] - kv_width
    groups = w_key_up.shape[0]
    head_width = w_query.shape[1] // groups
    nope_width = head_width - rope_width
    value_width = w_value_up.shape[2]
    score_scale = head_width ** (-0.5)
    block_width = cache_rows + fresh_rows
    ctx_index = lax.axis_index("ctx")
    local_tok = ctx_index * fresh_rows + jnp.arange(fresh_rows, dtype=jnp.int32)
    positions = (prefix_len[:, None] + local_tok[None, :]).astype(jnp.float32)
    features = lax.all_gather(query_compressed, "wt", axis=2, tiled=True)
    q_normed = rms_scale(features.astype(jnp.float32), query_gain).astype(jnp.bfloat16)
    q_full = jnp.dot(
        q_normed.reshape(prompts * fresh_rows, -1), w_query, preferred_element_type=jnp.float32
    )
    q_full = q_full.reshape(prompts, fresh_rows, groups, head_width)
    q_nope = q_full[..., :nope_width].astype(jnp.bfloat16)
    q_rope = rotate(jnp.swapaxes(q_full[..., nope_width:], 1, 2), positions[:, None, :]).astype(
        jnp.bfloat16
    )
    q_lat = jnp.einsum(
        "sqgd,gcd->sgqc",
        q_nope,
        lax.all_gather(w_key_up, "ctx", axis=1, tiled=True),
        preferred_element_type=jnp.float32,
    ).astype(jnp.bfloat16)
    latent_part = rms_scale(new_latent[..., :kv_width].astype(jnp.float32), latent_gain).astype(
        jnp.bfloat16
    )
    rope_part = rotate(new_latent[..., kv_width:].astype(jnp.float32), positions).astype(
        jnp.bfloat16
    )
    own_block = jnp.concatenate([cache, jnp.concatenate([latent_part, rope_part], -1)], 1)
    start_max = jnp.full((prompts, groups, fresh_rows), -1e30, jnp.float32)
    start_sum = jnp.zeros((prompts, groups, fresh_rows), jnp.float32)
    start_acc = jnp.zeros((prompts, groups, fresh_rows, kv_width), jnp.float32)
    initial = (start_max, start_sum, start_acc)
    portion = lax.all_gather(own_block, "ctx", axis=1, tiled=True)
    row_index = jnp.arange(portion.shape[1], dtype=jnp.int32)
    visible = visibility(
        row_index // block_width,
        row_index % block_width,
        cache_rows,
        fresh_rows,
        prefix_len,
        local_tok,
    )
    final = attend(initial, portion, visible, q_lat, q_rope, kv_width, score_scale)
    o_lat = (final[2] / final[1][..., None]).astype(jnp.bfloat16)
    output = jnp.einsum(
        "sgqc,gcv->sqgv",
        o_lat,
        lax.all_gather(w_value_up, "ctx", axis=1, tiled=True),
        preferred_element_type=jnp.float32,
    )
    return output.reshape(prompts, fresh_rows, groups * value_width).astype(jnp.bfloat16)


def solution(mesh):
    return jax.shard_map(
        shards,
        mesh=mesh,
        in_specs=(
            P(None, "ctx", "wt"),
            P(),
            P(None, ("wt", "head")),
            P(None, "ctx", None),
            P(),
            P(None, "ctx", None),
            P(),
            P(("wt", "head"), "ctx", None),
            P(("wt", "head"), "ctx", None),
        ),
        out_specs=P(None, "ctx", ("wt", "head")),
        check_vma=False,
    )
```

profile of v0, /device:TPU:4, one launch (start us, length us, event | category | flops | bytes accessed | tf_op | source)
XLA Modules:
  0.0 450.7 jit_solution(8158803665702589536)
XLA Ops:
  6.5 0.7 all-gather.4.cloned.1.call-update
  7.3 1.4 copy.18
  8.7 1.0 fusion.31
  9.7 0.7 add_convert_fusion.2
  10.5 0.8 slice_convert_fusion.3
  11.2 0.3 multiply_cosine_fusion
  11.5 1.0 fusion.33
  12.6 1.0 maximum_maximum_fusion
  13.7 0.7 all-gather.8.cloned.1.call-update
  14.5 7.9 %all_gather.12 = bf16[2,64,1536]{2,1,0:T(8,128)(2,1)S(1)} all-gather(bf16[2,64,384]{2,1,0:T(8,128)(2,1)} %param.9), channel_id=1, replica_groups=mesh['ctx'=16,'wt'=4,'head'=4] {'wt'}, dimensions={2}, use_global_device_ids=true | all-gather | bytes 491520 | tf_op jit(solution)/shard_map/all_gather | solution.py:82
  22.3 0.2 fusion.23
  22.5 6.7 %copy.17 = bf16[1536,1536]{0,1:T(8,128)(2,1)} copy(bf16[1536,1536]{1,0:T(8,128)(2,1)} %param.11) | data formatting | bytes 9437184 | tf_op args[2]
  29.2 4.1 fusion.27
  33.3 0.3 compare_and_fusion
  33.7 0.3 broadcast_or_fusion
  34.0 0.3 subtract_convert_fusion
  34.3 46.3 %all-gather.4.cloned.1.call-done = bf16[8,512,128]{2,1,0:T(8,128)(2,1)} async-done(((bf16[8,32,128]{2,1,0:T(8,128)(2,1)}), bf16[8,512,128]{2,1,0:T(8,128)(2,1)}) %all-gather.4.cloned.1.call-update) | async-done | bytes 1048592 | tf_op jit(solution)/shard_map/all_gather | solution.py:95
  80.6 279.6 %all-gather.6.cloned.1.call-done = bf16[2,5120,576]{2,1,0:T(8,128)(2,1)} async-done(((bf16[2,320,576]{2,1,0:T(8,128)(2,1)}), bf16[2,5120,576]{2,1,0:T(8,128)(2,1)}) %all-gather.6.cloned.1.call-update) | async-done | bytes 11796496 | tf_op jit(solution)/shard_map/all_gather | solution.py:109
  360.2 13.1 %fusion.2 = f32[2,8,64,5120]{3,2,1,0:T(8,128)} fusion(bf16[2,5120,576]{2,1,0:T(8,128)(2,1)} %all-gather.6.cloned.1.call-done, bf16[8,512,128]{2,1,0:T(8,128)(2,1)} %all-gather.4.cloned.1.call-done, f32[2,64,8,192]{3,1,2,0:T(8,128)S(1)} %fusion.27), kind=kOutput, calls=%fused_computation.4 | convolution fusion | flops 5503451136 | bytes 32768000 | tf_op jit(solution)/shard_map/sgqc,snc->sgqn/dot_general | solution.py:41
  373.3 14.4 %fusion.45 = (f32[2,8,64]{2,1,0:T(8,128)S(1)}, f32[2,8,64,5120]{3,2,1,0:T(8,128)}) fusion(f32[2,8,64,5120]{3,2,1,0:T(8,128)} %fusion.2, bf16[2,5120,576]{2,1,0:T(8,128)(2,1)} %all-gather.6.cloned.1.call-done, bf16[2,8,64,32]{3,2,1,0:T(8,128)(2,1)S(1)} %get-tuple-element.8, bf16[2,8,64,32]{3,2,1,0:T(8,128)(2,1)S(1)} %get-tuple-element.7, ...), kind=kOutput, calls=%fused_computation.72 | convolution fusion | flops 692321280 | bytes 45355008 | tf_op jit(solution)/shard_map/sgqr,snr->sgqn/dot_general | solution.py:42
  387.8 14.2 %fusion = (f32[2,8,64]{2,1,0:T(8,128)S(1)}, bf16[2,8,64,5120]{3,2,1,0:T(8,128)(2,1)}) fusion(f32[2,8,64,5120]{3,2,1,0:T(8,128)} %get-tuple-element.16, f32[2,8,64]{2,1,0:T(8,128)S(1)} %broadcast_maximum_fusion, pred[2,64,5120]{2,1,0:T(8,128)(4,1)S(1)} %broadcast_or_fusion), kind=kLoop, calls=%fused_computation.2 | loop fusion | flops 20970496 | bytes 32120832 | tf_op jit(solution)/shard_map/reduce_sum | solution.py:49
  402.0 31.0 %all-gather.8.cloned.1.call-done = bf16[8,512,128]{2,1,0:T(8,128)(2,1)} async-done(((bf16[8,32,128]{2,1,0:T(8,128)(2,1)}), bf16[8,512,128]{2,1,0:T(8,128)(2,1)}) %all-gather.8.cloned.1.call-update) | async-done | bytes 1048592 | tf_op jit(solution)/shard_map/all_gather | solution.py:124
  433.0 10.4 %fusion.14 = bf16[8,2,8,8,128]{4,3,2,1,0:T(8,128)(2,1)S(1)} fusion(bf16[2,5120,576]{2,1,0:T(8,128)(2,1)} %all-gather.6.cloned.1.call-done, bf16[2,8,64,5120]{3,2,1,0:T(8,128)(2,1)} %get-tuple-element.6, bf16[8,512,128]{2,1,0:T(8,128)(2,1)} %all-gather.8.cloned.1.call-done, f32[2,8,64]{2,0,1:T(2,128)S(1)} %copy.21), kind=kOutput, calls=%fused_computation.18 | convolution fusion | flops 5504106496 | bytes 22286336 | tf_op jit(solution)/shard_map/sgqc,gcv->sqgv/dot_general | solution.py:121
  443.4 0.8 copy.37
  (20 shorter events, 0.3 us)
Async XLA Ops:
  6.5 22.6 %copy-start = (f32[1536]{0:T(1024)S(1)}, f32[1536]{0:T(1024)}, u32[]{:S(2)}) copy-start(f32[1536]{0:T(1024)} %param.10) | copy-start | bytes 18436
  6.5 74.1 %all-gather.4.cloned.1.call-start = ((), (), s32[]{:S(2)}) async-start(), calls=%async_computation | async-start | bytes 1114112 | tf_op jit(solution)/shard_map/all_gather | solution.py:95
  7.3 353.0 %all-gather.6.cloned.1.call-start = ((), (), s32[]{:S(2)}) async-start(), calls=%async_computation.1 | async-start | bytes 13926400 | tf_op jit(solution)/shard_map/all_gather | solution.py:109
  11.2 22.3 %copy-start.1 = (s32[2]{0:T(128)S(1)}, s32[2]{0:T(128)}, u32[]{:S(2)}) copy-start(s32[2]{0:T(128)} %param.15) | copy-start | bytes 28
  13.6 419.3 %all-gather.8.cloned.1.call-start = ((), (), s32[]{:S(2)}) async-start(), calls=%async_computation.2 | async-start | bytes 1114112 | tf_op jit(solution)/shard_map/all_gather | solution.py:124
Sparse Core Ops, SparseCore 0:
  9.2 71.4 all-gather.3
  82.4 277.7 all-gather.5
  362.0 70.9 all-gather.7
where the time goes:
time: 451 us
  waiting for transfers between devices  358 us (79%)
  matrix products  42 us (9%)
  other arithmetic  20.2 us (4%)
  between operations  13.2 us (3%)
  local copies, waits for them, and re-layouts  8.86 us (2%)
  blocking collectives  7.87 us (2%)
    all_gather x1, waiting for transfers between devices, shards(): portion = lax.all_gather(own_block, 'ctx', axis=1, tiled=True)  280 us
    all_gather x1, waiting for transfers between devices, shards(): lax.all_gather(w_key_up, 'ctx', axis=1, tiled=True)  46.3 us
    all_gather x1, waiting for transfers between devices, shards(): lax.all_gather(w_value_up, 'ctx', axis=1, tiled=True)  31 us
    dot_general x1, matrix products, attend(): jnp.einsum('sgqr,snr->sgqn', q_rope, portion[..., kv_width:], preferred_e...  14.4 us
    reduce_sum x1, other arithmetic, attend(): weight_sum = jnp.sum(weights, axis=-1)  14.2 us
    dot_general x1, matrix products, attend(): jnp.einsum('sgqc,snc->sgqn', q_lat, latent, preferred_element_type=jnp.fl...  13.1 us
    dot_general x1, matrix products, shards(): jnp.einsum('sgqc,gcv->sqgv', o_lat, lax.all_gather(w_value_up, 'ctx', axi...  10.4 us
  transfers between devices with their start and end apart: 3, of which 3 were waited for; matrix products, arithmetic and copies ran while one was open for 13% of the time, Pallas kernels for 0%

commit v1 on v0

v1 whole, which is shorter than its diff:
```python
import jax
import jax.numpy as jnp
from jax import lax
from jax.experimental import pallas as pl
from jax.experimental.pallas import tpu as pltpu
from jax.sharding import PartitionSpec as P

MESH = pl.DeviceIdType.MESH
eps = 1e-06
rope_base = 10000.0
SLICE = 80
CUT = 48
KEYS = 8 * SLICE
NEG = -1e30
SCALE = 1.4426950408889634 * (192 ** -0.5)
ORDER = [0, -1, 1, -2, 2, -3, 3, 4]
DY = [0, -1, 1, 2]


def remote(src, dst, send_sem, recv_sem, device):
    return pltpu.make_async_remote_copy(
        src_ref=src, dst_ref=dst, send_sem=send_sem, recv_sem=recv_sem, device_id=device, device_id_type=MESH
    )


def kernel(
    qc_ref, gain_ref, wq_hbm, latent_ref, lgain_ref, cache_ref, cos_ref, sin_ref, thr_ref, wk_ref, wv_ref,
    out_ref,
    kown, kbuf, qcbuf, qn, wq, qmsg, qbuf, q_all, wmsg, wbuf, acc, top, osend,
    wqsem, lsem, xsem, zs, zr, ys, yr, cs, cr, qs, qr, ws, wr, wxsem, fsem, os, orr,
):
    ctx = lax.axis_index("ctx")
    wt = lax.axis_index("wt")
    y = lax.axis_index("head")
    z, xl, core = ctx // 2, ctx % 2, wt % 2
    e = core * 4 + y
    partner = (ctx + 1 - 2 * xl, wt, y)
    up = ((ctx + 2) % 16, wt, y)
    down = ((ctx + 14) % 16, wt, y)
    sib = (ctx, wt + 1 - 2 * core, y)
    far_wt = (wt + 2) % 4
    far = (ctx, far_wt, y)
    yup = (ctx, wt, (y + 1) % 4)
    ydown = (ctx, wt, (y + 3) % 4)

    wq_copy = pltpu.make_async_copy(wq_hbm, wq, wqsem)
    wq_copy.start()
    barrier = pltpu.get_barrier_semaphore()
    greeted = [((ctx + i) % 16, wt, y) for i in range(1, 16)] + [yup, ydown, sib, far]
    for device in greeted:
        pl.semaphore_signal(barrier, inc=1, device_id=device, device_id_type=MESH)

    lane = lax.broadcasted_iota(jnp.int32, (32, 128), 1)

    def rotated(part, s):
        twice = jnp.concatenate([part, part], axis=1)
        return twice * cos_ref[s] + pltpu.roll(twice, 32, 1) * sin_ref[s]

    for s in range(2):
        kown[s, 0:256, 0:512] = cache_ref[s, :, 0:512]
        tail = cache_ref[s, :, 512:576]
        kown[s, 0:256, 512:640] = jnp.concatenate([tail, tail], axis=1)
        lat = latent_ref[s, :, 0:512].astype(jnp.float32)
        lat = lat * lax.rsqrt(jnp.mean(lat * lat, axis=1, keepdims=True) + eps) * lgain_ref[...]
        kown[s, 256:320, 0:512] = lat.astype(jnp.bfloat16)
        kown[s, 256:320, 512:640] = rotated(latent_ref[s, :, 512:576].astype(jnp.float32), s).astype(jnp.bfloat16)
    qcbuf[wt] = qc_ref[...].reshape(128, 384)
    wmsg[:, :, 0:128] = wk_ref[...]
    wmsg[:, :, 128:256] = wv_ref[...]
    wbuf[z, xl] = wmsg[z]
    acc[...] = jnp.zeros_like(acc)
    top[...] = jnp.full_like(top, NEG)
    pl.semaphore_wait(barrier, len(greeted))

    pending = []

    def start(copy):
        copy.start()
        pending.append(copy)

    def qc_copy(owner, idx, device):
        return remote(qcbuf.at[owner], qcbuf.at[owner], fsem.at[0, idx], fsem.at[1, idx], device)

    start(qc_copy(wt, 0, far))
    start(qc_copy(wt, 1, sib))

    rows = pl.ds(pl.multiple_of(y * SLICE, 16), SLICE)
    mine = kbuf.at[z, e]
    own_k = pltpu.make_async_copy(kown.at[xl, rows], mine, lsem)
    x_copy = remote(kown.at[1 - xl, rows], mine, xsem.at[0], xsem.at[1], partner)

    @pl.when(xl == core)
    def _():
        x_copy.start()
        own_k.start()
        own_k.wait()

    @pl.when(xl != core)
    def _():
        x_copy.wait_recv()

    first, second = pl.ds(0, CUT), pl.ds(CUT, SLICE - CUT)

    def slot(b, dy, c):
        return kbuf.at[(z + ORDER[b] + 8) % 8, c * 4 + (y + dy + 4) % 4]

    def z_copy(b, direction, idx, part=None):
        ref = slot(b, 0, core)
        if part is not None:
            ref = ref.at[part]
        return remote(ref, ref, zs.at[idx], zr.at[idx], up if direction > 0 else down)

    def y_copy(b, dy, kind, part=None):
        ref = slot(b, dy, core)
        if part is not None:
            ref = ref.at[part]
        return remote(ref, ref, ys.at[b, kind], yr.at[b, kind], yup if kind % 2 == 0 else ydown)

    def c_copy(b, kind, c):
        ref = slot(b, DY[kind], c)
        return remote(ref, ref, cs.at[b, kind], cr.at[b, kind], sib)

    def begin(b):
        start(y_copy(b, 0, 0))
        start(y_copy(b, 0, 1))
        start(c_copy(b, 0, core))

    def middle(b):
        y_copy(b, -1, 0).wait_recv()
        start(y_copy(b, -1, 2, first))
        start(c_copy(b, 1, core))
        y_copy(b, 1, 1).wait_recv()
        start(y_copy(b, 1, 3, second))
        start(c_copy(b, 2, core))

    def finish(b):
        y_copy(b, 2, 2, first).wait_recv()
        y_copy(b, 2, 3, second).wait_recv()
        start(c_copy(b, 3, core))

    def arrive(b):
        direction = 1 if b % 2 == 1 else -1
        if b == 7:
            z_copy(b, 1, 6, first).wait_recv()
            z_copy(b, -1, 7, second).wait_recv()
        else:
            z_copy(b, direction, b - 1).wait_recv()
            if b < 5:
                start(z_copy(b, direction, b + 1))
            elif direction > 0:
                start(z_copy(b, direction, 6, first))
            else:
                start(z_copy(b, direction, 7, second))
        begin(b)

    start(z_copy(0, 1, 0))
    start(z_copy(0, -1, 1))
    begin(0)

    def w_copy(i):
        dest = (z + i) % 8
        return remote(wmsg.at[dest], wbuf.at[z, xl], ws.at[i], wr.at[i], (2 * dest + xl, wt, y))

    @pl.loop(1, 8)
    def _(i):
        w_copy(i).start()

    qc_copy(far_wt, 0, far).wait_recv()
    start(qc_copy(far_wt, 2, sib))
    sib_wt = wt + 1 - 2 * core
    qc_copy(sib_wt, 1, sib).wait_recv()
    arrive(1)
    arrive(2)
    qc_copy((sib_wt + 2) % 4, 2, sib).wait_recv()

    total = jnp.zeros((128, 1), jnp.float32)
    for k in range(4):
        part = qcbuf[k].astype(jnp.float32)
        total = total + jnp.sum(part * part, axis=1, keepdims=True)
    inverse = lax.rsqrt(total * (1.0 / 1536.0) + eps)
    for k in range(4):
        cols = slice(384 * k, 384 * k + 384)
        qn[:, cols] = (qcbuf[k].astype(jnp.float32) * inverse * gain_ref[:, cols]).astype(jnp.bfloat16)
    wq_copy.wait()

    def project(k):
        full = jnp.dot(qn[...], wq[:, 384 * k : 384 * k + 384], preferred_element_type=jnp.float32)
        for a in range(2):
            for s in range(2):
                tokens = full[64 * s : 64 * s + 64]
                d = 2 * (2 * k + a) + s
                qmsg[d, 0:64] = tokens[:, 192 * a : 192 * a + 128].astype(jnp.bfloat16)
                turned = rotated(tokens[:, 192 * a + 128 : 192 * a + 192], s)
                qmsg[d, 64:96] = jnp.where(lane < 64, turned[0:32], turned[32:64]).astype(jnp.bfloat16)

    project(0)
    project(1)
    middle(0)
    project(2)
    project(3)
    qbuf[ctx] = qmsg[ctx]

    def q_copy(i):
        dest = (ctx + i) % 16
        return remote(qmsg.at[dest], qbuf.at[ctx], qs.at[i], qr.at[i], (dest, wt, y))

    @pl.loop(1, 16)
    def _(i):
        q_copy(i).start()

    @pl.loop(1, 8)
    def _(i):
        src = (z + 8 - i) % 8
        remote(wmsg.at[0], wbuf.at[src, xl], ws.at[i], wr.at[i], partner).wait_recv()

    def wx_copy(half):
        return remote(wbuf.at[:, half], wbuf.at[:, half], wxsem.at[0], wxsem.at[1], partner)

    start(wx_copy(xl))

    arrive(3)
    arrive(4)
    finish(0)
    middle(1)
    middle(2)

    @pl.loop(1, 16)
    def _(i):
        src = (ctx + 16 - i) % 16
        remote(qmsg.at[0], qbuf.at[src], qs.at[i], qr.at[i], partner).wait_recv()

    for d in range(16):
        at = 64 * d
        q_all[at : at + 64, 0:128] = qbuf[d, 0:64]
        packed = qbuf[d, 64:96]
        zero = jnp.zeros_like(packed)
        q_all[at : at + 32, 128:256] = jnp.where(lane < 64, packed, zero)
        q_all[at + 32 : at + 64, 128:256] = jnp.where(lane < 64, zero, packed)
    wx_copy(1 - xl).wait_recv()

    def o_copy(d):
        piece = pl.ds(pl.multiple_of(d * 64, 64), 64)
        return remote(osend.at[piece], out_ref.at[ctx], os.at[d], orr.at[ctx], (d, wt, y))

    def attend(b):
        for kind in range(4):
            c_copy(b, kind, 1 - core).wait_recv()
        zz = (z + ORDER[b] + 8) % 8
        block = kbuf[zz].reshape(KEYS, 640)
        weight = wbuf[...].reshape(512, 256)
        kv = jnp.dot(block[:, :512], weight, preferred_element_type=jnp.float32)
        key = jnp.concatenate([kv[:, :128].astype(jnp.bfloat16), block[:, 512:]], axis=1)
        value = jnp.concatenate([kv[:, 128:].astype(jnp.bfloat16), jnp.ones((KEYS, 128), jnp.bfloat16)], axis=1)
        threshold = thr_ref[zz]
        for g in range(4):
            g_now = (g + z // 2) % 4
            group = pl.ds(pl.multiple_of(g_now * 256, 256), 256)
            scores = lax.dot_general(
                q_all[group, :], key, (((1,), (1,)), ((), ())), preferred_element_type=jnp.float32
            )
            token = g_now * 256 + lax.broadcasted_iota(jnp.int32, (256, 1), 0)
            scores = jnp.where(token >= threshold, scores, NEG)
            old = top[group, :]
            new = jnp.maximum(old, jnp.max(scores, axis=1, keepdims=True))
            weights = jnp.exp2((scores - new[:, :1]) * SCALE).astype(jnp.bfloat16)
            shrink = jnp.exp2((old - new) * SCALE)
            top[group, :] = new
            sums = acc[group, :] * jnp.concatenate([shrink, shrink], axis=1) + jnp.dot(
                weights, value, preferred_element_type=jnp.float32
            )
            if b < 7:
                acc[group, :] = sums
            else:
                osend[group, :] = (sums[:, :128] / sums[:, 128:]).astype(jnp.bfloat16)
                for i in range(4):
                    d = g_now * 4 + i

                    @pl.when(d != ctx)
                    def _(d=d):
                        o_copy(d).start()

    attend(0)
    arrive(5)
    arrive(6)
    finish(1)
    finish(2)
    middle(3)
    middle(4)
    attend(1)
    arrive(7)
    finish(3)
    finish(4)
    middle(5)
    middle(6)
    attend(2)
    middle(7)
    finish(5)
    finish(6)
    attend(3)
    finish(7)
    attend(4)
    attend(5)
    attend(6)
    attend(7)
    out_ref[ctx] = osend[pl.ds(pl.multiple_of(ctx * 64, 64), 64), :]

    for copy in pending:
        copy.wait_send()

    @pl.when(xl == core)
    def _():
        x_copy.wait_send()

    @pl.loop(1, 8)
    def _(i):
        w_copy(i).wait_send()

    @pl.loop(1, 16)
    def _(i):
        q_copy(i).wait_send()
        other = (ctx + i) % 16
        o_copy(other).wait_send()
        remote(osend.at[pl.ds(0, 64)], out_ref.at[other], os.at[other], orr.at[other], partner).wait_recv()


def shards(
    query_compressed, query_gain, w_query, new_latent, latent_gain, cache, prefix_len, w_key_up, w_value_up
):
    ctx = lax.axis_index("ctx")
    token = ctx * 64 + jnp.arange(64, dtype=jnp.int32)
    positions = (prefix_len[:, None] + token[None, :]).astype(jnp.float32)
    frequency = jnp.exp(jnp.arange(32, dtype=jnp.float32) * (-2.0 / 64) * jnp.log(jnp.float32(rope_base)))
    angles = positions[..., None] * frequency
    cosine, sine = jnp.cos(angles), jnp.sin(angles)
    cosine = jnp.concatenate([cosine] * 4, -1)
    sine = jnp.concatenate([-sine, sine] * 2, -1)

    n = jnp.arange(8 * KEYS, dtype=jnp.int32).reshape(8, 1, KEYS)
    owner = n // (4 * SLICE)
    row = n % (4 * SLICE)
    here = jnp.sum(jnp.where(jnp.arange(2) == ctx % 2, prefix_len, 0))
    threshold = jnp.where(row < 256, jnp.where(owner * 256 + row < here, -1, 1 << 20), owner * 64 + row - 256)

    vmem = pl.BlockSpec(memory_space=pltpu.VMEM)
    any_spec = pl.BlockSpec(memory_space=pl.ANY)
    dma = pltpu.SemaphoreType.DMA
    bf16, f32 = jnp.bfloat16, jnp.float32
    out = pl.pallas_call(
        kernel,
        out_shape=jax.ShapeDtypeStruct((16, 64, 128), bf16),
        in_specs=[vmem, vmem, any_spec] + [vmem] * 8,
        out_specs=vmem,
        scratch_shapes=[
            pltpu.VMEM((2, 320, 640), bf16),
            pltpu.VMEM((8, 8, SLICE, 640), bf16),
            pltpu.VMEM((4, 128, 384), bf16),
            pltpu.VMEM((128, 1536), bf16),
            pltpu.VMEM((1536, 1536), bf16),
            pltpu.VMEM((16, 96, 128), bf16),
            pltpu.VMEM((16, 96, 128), bf16),
            pltpu.VMEM((1024, 256), bf16),
            pltpu.VMEM((8, 32, 256), bf16),
            pltpu.VMEM((8, 2, 32, 256), bf16),
            pltpu.VMEM((1024, 256), f32),
            pltpu.VMEM((1024, 128), f32),
            pltpu.VMEM((1024, 128), bf16),
            dma, dma, dma((2,)), dma((8,)), dma((8,)), dma((8, 4)), dma((8, 4)), dma((8, 4)), dma((8, 4)),
            dma((16,)), dma((16,)), dma((8,)), dma((8,)), dma((2,)), dma((2, 3)), dma((16,)), dma((16,)),
        ],
        compiler_params=pltpu.CompilerParams(
            collective_id=0, has_side_effects=True, vmem_limit_bytes=50 * 1024 * 1024
        ),
        cost_estimate=pl.CostEstimate(flops=8 * 10**9, bytes_accessed=8 * 10**6, transcendentals=5 * 10**6),
        name="attention",
    )(
        query_compressed, query_gain.reshape(1, 1536), w_query, new_latent, latent_gain.reshape(1, 512), cache,
        cosine, sine, threshold, w_key_up, w_value_up,
    )
    return jnp.transpose(out.reshape(8, 2, 64, 128), (1, 2, 0, 3)).reshape(2, 64, 1024)


def solution(mesh):
    return jax.shard_map(
        shards,
        mesh=mesh,
        in_specs=(
            P(None, "ctx", "wt"),
            P(),
            P(None, ("wt", "head")),
            P(None, "ctx", None),
            P(),
            P(None, "ctx", None),
            P(),
            P(("wt", "head"), "ctx", None),
            P(("wt", "head"), "ctx", None),
        ),
        out_specs=P(None, "ctx", ("wt", "head")),
        check_vma=False,
    )
```

time: 451 us -> 79 us (0.18)
  waiting for transfers between devices: 358 us -> 0 us
  Pallas kernels: 0 us -> 68.3 us
  matrix products: 42 us -> 0 us
  other arithmetic: 20.2 us -> 3.26 us
  between operations: 13.2 us -> 0.05 us
  blocking collectives: 7.87 us -> 0 us
    all_gather x3 -> x0, waiting for transfers between devices: 357 us -> none  [the longest x1 280 us: shards(): portion = lax.all_gather(own_block, 'ctx', axis=1, tiled=True)]
    pallas_call x0 -> x1, Pallas kernels: none -> 68.3 us  [shards(): pl.pallas_call(kernel, out_shape=jax.ShapeDtypeStruct((16, 64, 128), bf16...]
    dot_general x4 -> x0, matrix products: 42 us -> none  [the longest x1 14.4 us: attend(): jnp.einsum('sgqr,snr->sgqn', q_rope, portion[..., kv_width:], preferred_e...]
    reduce_sum x3 -> x1, other arithmetic: 15.3 us -> 1.29 us  [shards(): here = jnp.sum(jnp.where(jnp.arange(2) == ctx % 2, prefix_len, 0))]
    all_gather x1 -> x0, blocking collectives: 7.87 us -> none  [shards(): features = lax.all_gather(query_compressed, 'wt', axis=2, tiled=True)]
  transfers between devices with their start and end apart: 3 -> 0, of which waited for: 3 -> 0; matrix products, arithmetic and copies ran while one was open for 13% -> 0% of each run, Pallas kernels for 0% -> 0%
where the time goes in v1:
time: 79 us; the launch traced here: 78.6 us
  Pallas kernels  68.3 us (86%)
  local copies, waits for them, and re-layouts  7 us (9%)
  other arithmetic  3.26 us (4%)
    pallas_call x1, Pallas kernels, shards(): pl.pallas_call(kernel, out_shape=jax.ShapeDtypeStruct((16, 64, 128), bf16...  68.3 us
    unnamed x11, local copies, waits for them, and re-layouts  5.52 us

profile of v1, /device:TPU:4, one launch (start us, length us, event | category | flops | bytes accessed | tf_op | source)
XLA Modules:
  0.0 78.6 jit_solution(4151528468164715377)
XLA Ops:
  0.0 1.3 %fusion.1 = s32[]{:T(128)} fusion(s32[2]{0:T(128)} %param.15, s32[]{:T(128)S(6)} %select_n.62), kind=kLoop, calls=%fused_computation.12 | loop fusion | flops 5 | bytes 16 | tf_op jit(solution)/shard_map/reduce_sum | solution.py:341
  1.3 0.7 add_convert_fusion
  2.0 0.7 reshape.168.gain_ref
  2.7 0.8 compare_select_fusion.1.thr_ref
  3.5 0.3 fusion
  3.8 0.2 pad_maximum_fusion
  4.0 1.4 %copy.10.cache_ref = bf16[2,256,576]{2,1,0:T(8,128)(2,1)S(1)} copy(bf16[2,256,576]{1,2,0:T(8,128)(2,1)} %param.14) | data formatting | bytes 1179648 | tf_op args[5]
  5.4 0.0 copy-start
  5.4 0.9 %copy-done = bf16[2,64,576]{2,1,0:T(8,128)(2,1)S(1)} copy-done((bf16[2,64,576]{2,1,0:T(8,128)(2,1)S(1)}, bf16[2,64,576]{2,1,0:T(8,128)(2,1)}, u32[]{:S(2)}) %copy-start) | copy-done | bytes 147480
  6.3 0.0 copy-start.1
  6.3 0.9 %copy-done.1 = bf16[2,64,384]{2,1,0:T(8,128)(2,1)S(1)} copy-done((bf16[2,64,384]{2,1,0:T(8,128)(2,1)S(1)}, bf16[2,64,384]{2,1,0:T(8,128)(2,1)}, u32[]{:S(2)}) %copy-start.1) | copy-done | bytes 98328
  7.2 0.0 copy-start.2
  7.2 0.8 %copy-done.2 = bf16[8,32,128]{2,1,0:T(8,128)(2,1)S(1)} copy-done((bf16[8,32,128]{2,1,0:T(8,128)(2,1)S(1)}, bf16[8,32,128]{2,1,0:T(8,128)(2,1)}, u32[]{:S(2)}) %copy-start.2) | copy-done | bytes 65560
  8.0 0.0 copy-start.3
  8.0 0.8 %copy-done.3 = bf16[8,32,128]{2,1,0:T(8,128)(2,1)S(1)} copy-done((bf16[8,32,128]{2,1,0:T(8,128)(2,1)S(1)}, bf16[8,32,128]{2,1,0:T(8,128)(2,1)}, u32[]{:S(2)}) %copy-start.3) | copy-done | bytes 65560
  8.8 0.0 copy-start.4
  8.9 0.7 copy-done.4
  9.5 68.3 %attention.1 = bf16[16,64,128]{2,1,0:T(8,128)(2,1)S(1)} custom-call(bf16[2,64,384]{2,1,0:T(8,128)(2,1)S(1)} %copy-done.1, f32[1,1536]{1,0:T(1,128)S(1)} %reshape.168.gain_ref, bf16[1536,1536]{1,0:T(8,128)(2,1)} %wq_hbm.1, bf16[2,64,576]{2,1,0:T(8,128)(2,1)S(1)} %copy-done, f32[1,512]{1,0:T(1,128)S(1)} %bitcast.9, bf16[2,256,576]{2,1,0:T(8,128)(2,1)S(1)} %copy.10.cache_ref, ...), custom_call_target="tpu_custom_call" | custom-call | flops 8000000000 | bytes 8000000 | tf_op jit(solution)/shard_map/attention/pallas_call | solution.py:348
  77.8 0.8 copy.14
  (2 shorter events, 0.0 us)
Async XLA Ops:
  5.4 0.9 %copy-start = (bf16[2,64,576]{2,1,0:T(8,128)(2,1)S(1)}, bf16[2,64,576]{2,1,0:T(8,128)(2,1)}, u32[]{:S(2)}) copy-start(bf16[2,64,576]{2,1,0:T(8,128)(2,1)} %latent_ref.1) | copy-start | bytes 442372
  6.3 0.9 %copy-start.1 = (bf16[2,64,384]{2,1,0:T(8,128)(2,1)S(1)}, bf16[2,64,384]{2,1,0:T(8,128)(2,1)}, u32[]{:S(2)}) copy-start(bf16[2,64,384]{2,1,0:T(8,128)(2,1)} %qc_ref.1) | copy-start | bytes 294916
  7.2 0.8 %copy-start.2 = (bf16[8,32,128]{2,1,0:T(8,128)(2,1)S(1)}, bf16[8,32,128]{2,1,0:T(8,128)(2,1)}, u32[]{:S(2)}) copy-start(bf16[8,32,128]{2,1,0:T(8,128)(2,1)} %wk_ref.1) | copy-start | bytes 196612
  8.0 0.8 %copy-start.3 = (bf16[8,32,128]{2,1,0:T(8,128)(2,1)S(1)}, bf16[8,32,128]{2,1,0:T(8,128)(2,1)}, u32[]{:S(2)}) copy-start(bf16[8,32,128]{2,1,0:T(8,128)(2,1)} %wv_ref.1) | copy-start | bytes 196612
  8.8 0.7 copy-start.4
